TPU v7x, 32 devices: a whole 2x2x4 slice. The times are simulated.
32 devices in a mesh: com: 8 (over z, x), arc: 4 (over y, core).
Axes of the slice: x: 2, y: 2, z: 4, core: 2. Of those that a mesh axis runs over, the one named last changes fastest.
Arguments:
- lfactor: float32 [16, 768, 768], P('com'), as said below
- links: float32 [16, 768, 4096], P('com', None, 'arc'), may hold values from -0.078125 to 0.078125
- usage: int32 [16, 4096], P('com', 'arc'), may hold values 0 or 1
- demands: bfloat16 [16, 768, 256], P('com'), may hold values from -6 to 6
- damping: float32 [4096], P('arc'), may hold values from 0.2 to 1
Outputs:
- schur: float32 [4096, 4096], P('com', 'arc')
- newton_y: float32 [4096, 256], P('arc')
- steps: float32 [16, 768, 256], P('com', None, 'arc')
Inputs may be any that keep to these rules, and one draw needn't show every extreme that they name: lfactor[k] is lower triangular with its diagonal between 1 and 2.
All inputs are finite; a program needn't handle non-finite values. No bound on the sum of `usage` on one device may be relied on, other than what follows from the above.
Results may differ from a plain program's by a relative error of at most 0.003.
Values may be sent and summed in bfloat16 or wider, within the bound.
No kernel may reach another device: no remote copies, remote signals or barrier semaphores. Data moves between devices by JAX's collectives and lax.ppermute only.
A program may use at most 192 MiB of HBM per device.

v0:
```python
from functools import partial

import jax
import jax.numpy as jnp
from jax import lax
from jax.sharding import PartitionSpec as P


def on_device(lfactor, links, usage, demands, damping):
    coupling = links * usage[:, None, :].astype(jnp.float32)
    solve_lower = jax.vmap(partial(jax.scipy.linalg.solve_triangular, lower=True))
    transformed = solve_lower(lfactor, coupling).astype(jnp.bfloat16)
    gathered = lax.all_gather(transformed, "arc", axis=2, tiled=True)
    arcs_total = gathered.shape[2]
    tile_width = transformed.shape[2]
    row_count = arcs_total // lax.axis_size("com")
    joined = jnp.concatenate([transformed, demands], axis=2)
    columns = lax.slice_in_dim(gathered, 0, lax.axis_size("com") * row_count, axis=2)
    assembled = lax.psum_scatter(
        jnp.einsum("kic,kit->ct", columns, joined, preferred_element_type=jnp.float32),
        "com",
        scatter_dimension=0,
        tiled=True,
    )
    schur_block = assembled[:, :tile_width]
    rhs_rows = assembled[:, tile_width:]
    local_product = jnp.dot(schur_block.T, rhs_rows, precision=lax.Precision.HIGHEST)
    local_tile = jnp.einsum("kic,kip->cp", transformed, demands, preferred_element_type=jnp.float32)
    product, rhs_tile = lax.psum((local_product, local_tile), "com")
    newton_y = rhs_tile - damping[:, None] * product
    rounded_y = newton_y.astype(jnp.bfloat16)
    partial_terms = jnp.einsum(
        "kit,tp->kip", transformed, rounded_y, preferred_element_type=jnp.float32
    )
    corrections = lax.psum_scatter(
        partial_terms.astype(jnp.bfloat16), "arc", scatter_dimension=2, tiled=True
    ).astype(jnp.float32)
    share_width = corrections.shape[2]
    demand_share = lax.dynamic_slice_in_dim(
        demands, lax.axis_index("arc") * share_width, share_width, 2
    ).astype(jnp.float32)
    solve_upper = jax.vmap(partial(jax.scipy.linalg.solve_triangular, lower=True, trans=1))
    steps = solve_upper(lfactor, demand_share - corrections)
    return (schur_block, newton_y, steps)


def solution(mesh):
    in_specs = (
        P("com", None, None),
        P("com", None, "arc"),
        P("com", "arc"),
        P("com", None, None),
        P("arc"),
    )
    out_specs = (P("com", "arc"), P("arc", None), P("com", None, "arc"))
    return jax.shard_map(
        on_device, mesh=mesh, in_specs=in_specs, out_specs=out_specs, check_vma=False
    )
```

profile of v0, /device:TPU:0, one launch (start us, length us, event | category | flops | bytes accessed | tf_op | source)
XLA Modules:
  0.0 784.5 jit_solution(13468818099401690990)
XLA Ops:
  7.2 0.2 iota_compare_fusion
  7.4 5.1 broadcast_select_fusion
  12.5 17.8 %while.1 = (s32[]{:T(128)}, f32[2,768,768]{2,1,0:T(8,128)}, s32[6,2]{0,1:T(2,128)S(1)}, f32[6,2,128,128]{3,2,0,1:T(8,128)S(1)}, s32[]{:T(128)}) while((s32[]{:T(128)}, f32[2,768,768]{2,1,0:T(8,128)}, s32[6,2]{0,1:T(2,128)S(1)}, f32[6,2,128,128]{3,2,0,1:T(8,128)S(1)}, s32[]{:T(128)}) %tuple.29), condition=%wide.while_cond, body=%wide.while_body.sunk | while | flops 2 | bytes 262253 | solution.py:12
  12.5 0.1 constant_dynamic-slice_fusion.3
  12.6 0.5 fusion.100
  13.1 2.4 bitcast_dynamic-update-slice_fusion.2
  15.5 0.1 constant_dynamic-slice_fusion.3
  15.5 0.5 fusion.100
  16.1 2.4 bitcast_dynamic-update-slice_fusion.2
  18.4 0.1 constant_dynamic-slice_fusion.3
  18.5 0.5 fusion.100
  19.0 2.4 bitcast_dynamic-update-slice_fusion.2
  21.5 0.5 fusion.100
  22.0 2.4 bitcast_dynamic-update-slice_fusion.2
  24.4 0.1 constant_dynamic-slice_fusion.3
  24.5 0.5 fusion.100
  25.0 2.4 bitcast_dynamic-update-slice_fusion.2
  27.4 0.1 constant_dynamic-slice_fusion.3
  27.4 0.5 fusion.100
  28.0 2.3 bitcast_dynamic-update-slice_fusion.2
  30.3 118.6 %custom-call.7 = f32[2,6,128,128]{2,3,1,0:T(8,128)} custom-call(f32[2,6,128,128]{3,2,1,0:T(8,128)S(1)} %bitcast.75), custom_call_target="InvertDiagBlocksLowerTriangular" | custom-call | tf_op jit(solution)/shard_map/vmap(jit(_solve_triangular))/triangular_solve | solution.py:12
  148.9 3.6 broadcast_multiply_fusion
  152.5 1.1 convert_dynamic-update-slice_fusion.4
  153.5 1.9 convolution_subtract_fusion.1
  155.5 0.1 constant_dynamic-update-slice_fusion.4
  155.6 1.1 convert_dynamic-update-slice_fusion.3
  156.7 2.3 fusion.21
  159.0 1.1 convert_dynamic-update-slice_fusion.2
  160.1 3.1 fusion.24
  163.3 1.1 convert_dynamic-update-slice_fusion.1
  164.4 3.8 fusion.27
  168.2 1.1 convert_dynamic-update-slice_fusion
  169.3 0.1 constant_dynamic-update-slice_fusion
  169.4 4.3 convolution_subtract_fusion
  173.7 1.1 fusion.30
  174.8 1.6 copy-done.1
  176.5 84.9 %all-gather.2.cloned.1.call-done = bf16[2,768,4096]{2,1,0:T(8,128)(2,1)} async-done(((bf16[2,768,1024]{2,1,0:T(8,128)(2,1)}), bf16[2,768,4096]{2,1,0:T(8,128)(2,1)}) %all-gather.2.cloned.1.call-update) | async-done | bytes 12582928 | tf_op jit(solution)/shard_map/all_gather | solution.py:13
  261.4 22.8 %convolution_bitcast_fusion = f32[4096,1280]{1,0:T(8,128)} fusion(bf16[2,768,4096]{2,1,0:T(8,128)(2,1)} %all-gather.2.cloned.1.call-done, bf16[2,768,256]{2,1,0:T(8,128)(2,1)} %param.8, bf16[2,768,1024]{2,1,0:T(8,128)(2,1)} %copy-done.1), kind=kOutput, calls=%fused_computation.2 | convolution fusion | flops 16113991680 | bytes 37486592 | tf_op jit(solution)/shard_map/kic,kit->ct/dot_general | solution.py:20
  284.3 0.3 all-reduce.3.cloned.1.call-start
  284.5 1.6 copy-done.2
  286.1 3.1 convolution_bitcast_fusion.1
  289.2 338.7 %reduce-scatter.3.cloned.1.call-done = f32[512,1280]{1,0:T(8,128)} async-done(((f32[4096,1280]{1,0:T(8,128)}), f32[512,1280]{1,0:T(8,128)}) %reduce-scatter.3.cloned.1.call-update) | async-done | bytes 2621456 | tf_op jit(solution)/shard_map/reduce_scatter | solution.py:19
  627.9 1.7 slice.123
  629.6 5.9 fusion.36
  635.6 101.5 %all-reduce.3.cloned.1.call-done = (f32[1024,256]{1,0:T(8,128)}, f32[1024,256]{1,0:T(8,128)}) async-done(((f32[1024,256]{1,0:T(8,128)}, f32[1024,256]{1,0:T(8,128)}), (f32[1024,256]{1,0:T(8,128)}, f32[1024,256]{1,0:T(8,128)})) %all-reduce.3.cloned.1.call-update) | async-done | bytes 2097168 | tf_op jit(solution)/shard_map/psum | solution.py:29
  737.0 1.7 multiply_subtract_fusion
  738.8 1.0 copy-done.5
  739.8 3.9 convolution_convert_fusion
  743.7 1.2 constant_dynamic-slice_fusion.1
  744.9 0.2 copy.43
  745.0 21.8 %reduce-scatter.5.cloned.1.call-done = bf16[2,768,64]{1,2,0:T(8,128)(2,1)} async-done(((bf16[2,768,256]{1,2,0:T(8,128)(2,1)}), bf16[2,768,64]{1,2,0:T(8,128)(2,1)}) %reduce-scatter.5.cloned.1.call-update) | async-done | bytes 196624 | tf_op jit(solution)/shard_map/reduce_scatter | solution.py:35
  766.9 1.0 convert_subtract_fusion
  767.9 0.4 fusion.70
  768.2 1.2 convolution_subtract_fusion.4
  769.4 0.4 fusion.68
  769.7 1.3 convolution_subtract_fusion.5
  771.0 0.4 fusion.66
  771.4 1.4 convolution_subtract_fusion.6
  772.8 0.4 fusion.64
  773.1 1.5 convolution_subtract_fusion.3
  774.7 0.4 constant_dynamic-update-slice_fusion.9
  775.1 1.7 convolution_subtract_fusion.2
  776.8 0.4 convolution_dynamic-update-slice_fusion
  777.2 0.7 copy-done.6
  (38 shorter events, 0.6 us)
Async XLA Ops:
  7.2 254.3 %all-gather.2.cloned.1.call-start = ((), (), s32[]{:S(2)}) async-start(), calls=%async_computation.2 | async-start | bytes 15728640 | tf_op jit(solution)/shard_map/all_gather | solution.py:13
  7.4 141.4 %copy-start.7 = (s32[2,1024]{1,0:T(2,128)S(1)}, s32[2,1024]{1,0:T(2,128)}, u32[]{:S(2)}) copy-start(s32[2,1024]{1,0:T(2,128)} %param.7) | copy-start | bytes 24580
  148.9 3.6 copy-start.3
  174.8 1.6 copy-start.1
  176.5 451.4 %reduce-scatter.3.cloned.1.call-start = ((), (), s32[]{:S(2)}) async-start(), calls=%async_computation.3 | async-start | bytes 23592960 | tf_op jit(solution)/shard_map/reduce_scatter | solution.py:19
  284.2 1.9 copy-start.2
  284.3 452.8 %all-reduce.3.cloned.1.call-start = ((), (), s32[]{:S(2)}) async-start(), calls=%async_computation.5 | async-start | bytes 4194304 | tf_op jit(solution)/shard_map/psum | solution.py:29
  289.2 447.8 %copy-start.8 = (f32[1024]{0:T(1024)S(1)}, f32[1024]{0:T(1024)}, u32[]{:S(2)}) copy-start(f32[1024]{0:T(1024)} %param.9) | copy-start | bytes 12292
  629.6 114.0 %copy-start = (f32[512,1024]{1,0:T(8,128)}, f32[512,1024]{1,0:T(8,128)S(1)}, u32[]{:S(2)}) copy-start(f32[512,1024]{1,0:T(8,128)S(1)} %slice.123) | copy-start | bytes 6291460
  635.5 131.3 %reduce-scatter.5.cloned.1.call-start = ((), (), s32[]{:S(2)}) async-start(), calls=%async_computation.4 | async-start | bytes 983040 | tf_op jit(solution)/shard_map/reduce_scatter | solution.py:35
  738.8 1.0 copy-start.5
  739.8 28.1 %copy-start.4 = (f32[2,6,128,128]{2,3,1,0:T(8,128)S(1)}, f32[2,6,128,128]{2,3,1,0:T(8,128)}, u32[]{:S(2)}) copy-start(f32[2,6,128,128]{2,3,1,0:T(8,128)} %custom-call.7) | copy-start | bytes 2359300
  777.2 0.7 copy-start.6
Sparse Core Ops, SparseCore 0:
  176.6 84.7 all-gather.1
  284.4 343.4 reduce-scatter.2
  635.7 101.3 all-reduce.2
  743.8 23.0 reduce-scatter.4
where the time goes:
time: 786 us; the launch traced here: 784 us
  waiting for transfers between devices  547 us (70%)
  other arithmetic  130 us (17%)
  matrix products  66.6 us (8%)
  local copies, waits for them, and re-layouts  26.2 us (3%)
  between operations  14.2 us (2%)
    reduce_scatter x1, waiting for transfers between devices, on_device(): lax.psum_scatter(jnp.einsum('kic,kit->ct', columns, joined, preferred_ele...  339 us
    another operation x4, other arithmetic, on_device(): transformed = solve_lower(lfactor, coupling).astype(jnp.bfloat16)  124 us
    psum x1, waiting for transfers between devices, on_device(): product, rhs_tile = lax.psum((local_product, local_tile), 'com')  101 us
    all_gather x1, waiting for transfers between devices, on_device(): gathered = lax.all_gather(transformed, 'arc', axis=2, tiled=True)  84.9 us
    dot_general x1, matrix products, on_device(): jnp.einsum('kic,kit->ct', columns, joined, preferred_element_type=jnp.flo...  22.8 us
    reduce_scatter x1, waiting for transfers between devices, on_device(): lax.psum_scatter(partial_terms.astype(jnp.bfloat16), 'arc', scatter_dimen...  21.8 us
    another operation x11, matrix products, on_device(): transformed = solve_lower(lfactor, coupling).astype(jnp.bfloat16)  21.8 us
    another operation x18, local copies, waits for them, and re-layouts  17.7 us
  transfers between devices with their start and end apart: 4, of which 4 were waited for; matrix products, arithmetic and copies ran while one was open for 1% of the time, Pallas kernels for 0%

commit v1 on v0

v1 whole, which is shorter than its diff:
```python
import jax, jax.numpy as jnp
from jax import lax
from jax.experimental import pallas as pl
from jax.experimental.pallas import tpu as pltpu
from jax.sharding import PartitionSpec as P

BLOCK = 128
LEAF = 16

def halves(value):
    high = value.astype(jnp.bfloat16)
    low = (value - high.astype(jnp.float32)).astype(jnp.bfloat16)
    return high, low

def dot(a, b):
    return jnp.dot(a, b, preferred_element_type=jnp.float32)

def dot3(a, b):
    return dot(a[0], b[0]) + (dot(a[0], b[1]) + dot(a[1], b[0]))

def tdot(a, b):
    return lax.dot_general(a, b, (((0,), (0,)), ((), ())), preferred_element_type=jnp.float32)

def leaf_inverses(packed):
    rows, lanes = packed.shape
    lane = lax.broadcasted_iota(jnp.int32, (rows, lanes), 1)
    row = lax.broadcasted_iota(jnp.int32, (rows, lanes), 0) % LEAF
    inverse = (lane % LEAF == row).astype(jnp.float32)
    groups = rows // LEAF
    first = lane // LEAF * LEAF
    for step in range(LEAF):
        column = jnp.take_along_axis(packed, first + step, axis=1, mode="promise_in_bounds")
        def at_step(a):
            picked = a.reshape(groups, LEAF, lanes)[:, step : step + 1, :]
            return jnp.broadcast_to(picked, (groups, LEAF, lanes)).reshape(rows, lanes)
        done = at_step(inverse) / at_step(column)
        inverse = jnp.where(row > step, inverse - column * done, jnp.where(row == step, done, inverse))
    return inverse

def block_inverses(blocks):
    size = BLOCK
    lane = lax.broadcasted_iota(jnp.int32, (LEAF, size), 1)
    def pack(block):
        out = jnp.zeros((LEAF, size), jnp.float32)
        for part in range(size // LEAF):
            out = jnp.where(lane // LEAF == part, block[part * LEAF : (part + 1) * LEAF, :], out)
        return out
    leaves = leaf_inverses(jnp.concatenate([pack(b) for b in blocks], axis=0))
    inverses = []
    for index in range(len(blocks)):
        leaf = leaves[index * LEAF : (index + 1) * LEAF]
        inverses.append(jnp.concatenate(
            [jnp.where(lane // LEAF == part, leaf, 0.0) for part in range(size // LEAF)], axis=0))
    width = LEAF
    while width < size:
        parts = [(p, p + width) for p in range(width, size, 2 * width)]
        out = []
        for block, inverse in zip(blocks, inverses):
            odd = jnp.concatenate([inverse[p:q] for p, q in parts], axis=0)
            low = []
            for p, q in parts:
                spot = lax.broadcasted_iota(jnp.int32, (width, size), 1)
                low.append(jnp.where((spot >= p - width) & (spot < p), block[p:q], 0.0))
            low = jnp.concatenate([jnp.concatenate([jnp.zeros_like(l), l], axis=0) for l in low], axis=0)
            term = dot3(halves(odd), halves(low))
            term = dot3(halves(term), halves(inverse))
            pieces = []
            for number, (p, q) in enumerate(parts):
                pieces += [inverse[p - width : p], inverse[p:q] - term[number * width : (number + 1) * width]]
            out.append(jnp.concatenate(pieces, axis=0))
        inverses = out
        width *= 2
    return inverses

def forward_kernel(factor_ref, links_ref, usage_ref, demands_ref, out_ref, inverse_ref, rhs_ref, high_ref, low_ref):
    coms, nodes, _ = factor_ref.shape
    count = nodes // BLOCK
    span = lambda i: slice(i * BLOCK, (i + 1) * BLOCK)

    @pl.when(pl.program_id(0) == 0)
    def _():
        blocks = [factor_ref[c, span(i), span(i)] for c in range(coms) for i in range(count)]
        inverses = block_inverses(blocks)
        for c in range(coms):
            for i in range(count):
                inverse_ref[c, span(i)] = inverses[c * count + i]
            high, low = halves(factor_ref[c])
            high_ref[c] = high
            low_ref[c] = low

    solved = [[] for _ in range(coms)]
    for i in range(count):
        for c in range(coms):
            rest = links_ref[c, span(i)] * usage_ref[c].astype(jnp.float32)
            if i:
                high = jnp.concatenate([h for h, _ in solved[c]], axis=0)
                low = jnp.concatenate([l for _, l in solved[c]], axis=0)
                rest = rest - dot3((high_ref[c, span(i), : i * BLOCK], low_ref[c, span(i), : i * BLOCK]), (high, low))
            value = dot3(halves(inverse_ref[c, span(i)]), halves(rest))
            solved[c].append(halves(value))
            out_ref[c * nodes + i * BLOCK : c * nodes + (i + 1) * BLOCK] = solved[c][-1][0]
    rhs_ref[...] = sum(
        tdot(demands_ref[c], jnp.concatenate([h for h, _ in solved[c]], axis=0)) for c in range(coms))

def forward_solve(factor, links, usage, demands, tile=512):
    coms, nodes, arcs = links.shape
    scens = demands.shape[2]
    tile = min(tile, arcs)
    return pl.pallas_call(
        forward_kernel,
        grid=(arcs // tile,),
        in_specs=[
            pl.BlockSpec((coms, nodes, nodes), lambda t: (0, 0, 0)),
            pl.BlockSpec((coms, nodes, tile), lambda t: (0, 0, t)),
            pl.BlockSpec((coms, 1, tile), lambda t: (0, 0, t)),
            pl.BlockSpec((coms, nodes, scens), lambda t: (0, 0, 0)),
        ],
        out_specs=[
            pl.BlockSpec((coms * nodes, tile), lambda t: (0, t)),
            pl.BlockSpec((coms, nodes, BLOCK), lambda t: (0, 0, 0)),
            pl.BlockSpec((scens, tile), lambda t: (0, t)),
        ],
        out_shape=[
            jax.ShapeDtypeStruct((coms * nodes, arcs), jnp.bfloat16),
            jax.ShapeDtypeStruct((coms, nodes, BLOCK), jnp.float32),
            jax.ShapeDtypeStruct((scens, arcs), jnp.float32),
        ],
        scratch_shapes=[pltpu.VMEM((coms, nodes, nodes), jnp.bfloat16)] * 2,
        compiler_params=pltpu.CompilerParams(vmem_limit_bytes=48 * 2**20),
        cost_estimate=pl.CostEstimate(flops=6 * coms * nodes * nodes * arcs, bytes_accessed=4 * coms * nodes * (nodes + arcs) + 2 * coms * nodes * arcs, transcendentals=0),
    )(factor, links, usage.reshape(coms, 1, arcs), demands)

def backward_kernel(factor_ref, inverse_ref, demand_ref, correction_ref, out_ref):
    coms, nodes, _ = factor_ref.shape
    count = nodes // BLOCK
    span = lambda i: slice(i * BLOCK, (i + 1) * BLOCK)
    solved = [[] for _ in range(coms)]
    for i in reversed(range(count)):
        for c in range(coms):
            rest = demand_ref[c, span(i)].astype(jnp.float32).T - correction_ref[:, c * nodes + i * BLOCK : c * nodes + (i + 1) * BLOCK]
            if solved[c]:
                high = jnp.concatenate([h for h, _ in solved[c]], axis=1)
                low = jnp.concatenate([l for _, l in solved[c]], axis=1)
                rest = rest - dot3((high, low), halves(factor_ref[c, (i + 1) * BLOCK :, span(i)]))
            value = dot3(halves(rest), halves(inverse_ref[c, span(i)]))
            solved[c].insert(0, halves(value))
            out_ref[c, span(i)] = value.T

def backward_solve(factor, inverse, demand, correction):
    coms, nodes, scens = demand.shape
    return pl.pallas_call(
        backward_kernel,
        out_shape=jax.ShapeDtypeStruct((coms, nodes, scens), jnp.float32),
        compiler_params=pltpu.CompilerParams(vmem_limit_bytes=48 * 2**20),
    )(factor, inverse, demand, correction)

def times_kernel(*refs):
    *pieces, value_ref, out_ref = refs
    total = 0.0
    for number, piece in enumerate(pieces):
        total += lax.dot_general(value_ref[number], piece[...], (((1,), (1,)), ((), ())), preferred_element_type=jnp.float32)
    out_ref[...] = total

def project_kernel(*refs):
    *pieces, value_ref, out_ref = refs
    scens = value_ref.shape[0]
    both = jnp.concatenate(halves(value_ref[...]), axis=0)
    for number, piece in enumerate(pieces):
        found = dot(both, piece[...])
        out_ref[number] = found[:scens] + found[scens:]

def piece_call(kernel, pieces, value, shape):
    depth, columns = pieces[0].shape
    scens = value.shape[-2]
    return pl.pallas_call(
        kernel,
        out_shape=jax.ShapeDtypeStruct(shape, jnp.float32),
        compiler_params=pltpu.CompilerParams(vmem_limit_bytes=48 * 2**20),
        cost_estimate=pl.CostEstimate(flops=2 * len(pieces) * depth * columns * scens, bytes_accessed=2 * len(pieces) * depth * columns, transcendentals=0),
    )(*pieces, value)


def bit_count(size):
    return size.bit_length() - 1


def swap(value, axis, bits):
    size = lax.axis_size(axis)
    return lax.ppermute(value, axis, [(i, i ^ bits) for i in range(size)])


def pick(value, index, dim=0):
    return lax.dynamic_index_in_dim(value, index, dim, keepdims=False)


def wide(value):
    return value.astype(jnp.float32)


def after(value, *others):
    return lax.optimization_barrier((value, *others))[0]


class Link:

    def __init__(self, window=2):
        self.window = window
        self.results = []

    def send(self, values, axis, bits):
        if len(self.results) >= self.window:
            values = lax.optimization_barrier((tuple(values), self.results[-self.window]))[0]
        got = [swap(value, axis, bit) for value, bit in zip(values, bits)]
        self.results.append(got)
        return got


def on_device(lfactor, links, usage, demands, damping):
    place, arc = lax.axis_index("com"), lax.axis_index("arc")
    coms, arcs = lax.axis_size("com"), lax.axis_size("arc")
    side, outer, outers = place % 2, place // 2, coms // 2
    steps_out = range(1, outers)
    far_bits = [2 * step for step in steps_out]
    over_y, over_x, over_z = Link(), Link(), Link()

    def send_x(value):
        return over_x.send([value], "com", [1])[0]

    def send_z(values):
        return over_z.send(values, "com", far_bits)

    def send_y(values, bits):
        return over_y.send(values, "arc", bits)

    panel, inverse, local = forward_solve(lfactor, links, usage, demands)
    count, nodes, _ = lfactor.shape
    depth, width = panel.shape
    scens = demands.shape[2]
    share = scens // arcs
    chunks = arcs
    pairs = outers // chunks
    rows = width // coms
    span = pairs * rows
    halves_of = range(arcs // 2)

    def columns_of(value, which, chunk):
        starts = [((j * 2 + which) * chunks + chunk) * rows for j in range(pairs)]
        parts = [lax.dynamic_slice_in_dim(value, start, rows, value.ndim - 1) for start in starts]
        return jnp.concatenate(parts, axis=-1)

    own = [jnp.concatenate([columns_of(panel, 1 - side, n), columns_of(panel, side, n)], axis=1) for n in range(chunks)]
    lead, rest = {}, {}

    def split(chunk, half, first, second):
        lead[half, chunk] = jnp.concatenate([first[:, :span], second[:, :span]], axis=1)
        rest[half, chunk] = jnp.concatenate([first[:, span:], second[:, span:]], axis=1)

    def fetch_near(chunk):
        split(chunk, 0, own[chunk], swap(own[chunk], "arc", 1))

    def fetch_far(chunk):
        (got,) = send_y([own[chunk]], [2])
        split(chunk, 1, got, swap(got, "arc", 1))

    got_x = {}

    def schur_x(half, chunk):
        got_x[half, chunk] = send_x(tdot(lead[half, chunk], panel).astype(jnp.bfloat16))

    schur_out = [None] * chunks

    def schur_z(chunk):
        total = jnp.concatenate([tdot(rest[h, chunk], panel) + wide(got_x[h, chunk]) for h in halves_of])
        total = total.reshape(arcs, pairs, rows, width)
        def block_for(step):
            to = outer ^ step
            return pick(pick(total, arc ^ (to // pairs)), to % pairs)
        got = send_z([block_for(step).astype(jnp.bfloat16) for step in steps_out])
        schur_out[chunk] = sum((wide(g) for g in got), block_for(0))

    def reduce_outer(total):
        def part(owner):
            return lax.dynamic_slice_in_dim(pick(total, owner % chunks), owner // chunks * rows, rows, total.ndim - 2)
        got = send_z([part(outer ^ step) for step in steps_out])
        return sum(got, part(outer))

    def spread(value):
        held = jnp.stack([value] + send_z([value for _ in steps_out]))
        owners = [pick(held, outer ^ n) for n in range(outers)]
        near = jnp.stack([jnp.concatenate(owners[n::chunks], axis=-1) for n in range(chunks)])
        return send_x(near), near

    def paired(value):
        return jnp.stack([jnp.concatenate([value[n, 2 * h], value[n, 2 * h + 1]], axis=1) for h, n in rest])

    def times(far, near):
        found = piece_call(times_kernel, list(rest.values()), paired(near), (share, depth))
        return found + piece_call(times_kernel, [lead[k] for k in rest], paired(far), (share, depth))

    def project(pieces, inner):
        found = piece_call(project_kernel, list(pieces.values()), inner, (len(pieces), share, 2 * span))
        found = {k: found[n] for n, k in enumerate(pieces)}
        return jnp.stack([
            jnp.stack([found[h, n][:, p * span : (p + 1) * span] for h in halves_of for p in range(2)]) for n in range(chunks)])

    def of_side(which):
        return jnp.stack([columns_of(local, which, n) for n in range(chunks)])
    total = of_side(side) + send_x(of_side(1 - side))
    fetch_far(0)
    fetch_near(0)
    schur_x(0, 0)
    fetch_far(1)
    own_rhs = reduce_outer(total)
    fetch_near(1)
    schur_x(0, 1)
    slices = own_rhs.reshape(arcs, share, rows)
    others = range(1, arcs)
    rhs = jnp.stack([pick(slices, arc)] + [swap(pick(slices, arc ^ m), "arc", m) for m in others])
    own_damping = pick(pick(damping.reshape(pairs, 2, chunks, rows), side, 1).reshape(outers, rows), outer)
    damp = jnp.stack([own_damping] + [swap(own_damping, "arc", m) for m in others])
    fetch_far(2)
    schur_x(1, 0)
    fetch_near(2)
    fetch_near(3)
    fetch_far(3)
    inner = times(*spread(rhs.astype(jnp.bfloat16)))
    schur_x(0, 2)
    schur_z(0)
    schur_x(1, 1)
    schur_z(1)
    other = send_x(project(lead, inner))
    total = project(rest, inner) + other
    schur_x(0, 3)
    product = reduce_outer(total)
    schur_x(1, 2)
    schur_z(2)
    newton = rhs - damp[:, None, :] * product
    far_y, near_y = spread(newton.astype(jnp.bfloat16))
    schur_x(1, 3)
    schur_z(3)
    corrections = times(far_y, near_y)
    demand_share = lax.dynamic_slice_in_dim(demands, arc * share, share, 2)
    steps = backward_solve(lfactor, inverse, demand_share, corrections)

    def home(m):
        parts = [[jnp.where(side == which, near_y[n, m], far_y[n, m]) for n in range(chunks)] for which in range(2)]
        return jnp.concatenate([
            parts[which][n][:, j * rows : (j + 1) * rows]
            for j in range(pairs) for which in range(2) for n in range(chunks)], axis=1)
    held = jnp.stack([home(0)] + [swap(home(m), "arc", m) for m in others])
    newton_y = wide(jnp.concatenate([pick(held, arc ^ n) for n in range(arcs)])).T
    return (jnp.concatenate(schur_out, axis=0), newton_y, steps)


def solution(mesh):
    in_specs = (
        P("com", None, None),
        P("com", None, "arc"),
        P("com", "arc"),
        P("com", None, None),
        P("arc"),
    )
    out_specs = (P("com", "arc"), P("arc", None), P("com", None, "arc"))
    return jax.shard_map(
        on_device, mesh=mesh, in_specs=in_specs, out_specs=out_specs, check_vma=False
    )
```

time: 786 us -> 342 us (0.44)
  waiting for transfers between devices: 547 us -> 139 us
  other arithmetic: 130 us -> 31.1 us
  starting transfers between devices: 0.38 us -> 77.9 us
  matrix products: 66.6 us -> 25.2 us
  Pallas kernels: 0 us -> 38.8 us
  between operations: 14.2 us -> 2.64 us
    reduce_scatter x2 -> x0, waiting for transfers between devices: 361 us -> none  [the longest x1 339 us: on_device(): lax.psum_scatter(jnp.einsum('kic,kit->ct', columns, joined, preferred_ele...]
    ppermute x0 -> x57, waiting for transfers between devices: none -> 139 us  [swap(): return lax.ppermute(value, axis, [(i, i ^ bits) for i in range(size)])]
    another operation x4 -> x24, other arithmetic: 124 us -> 3.75 us  [the longest x1 1.28 us: on_device(): jnp.stack([own_damping] + [swap(own_damping, 'arc', m) for m in others])]
    psum x1 -> x0, waiting for transfers between devices: 101 us -> none  [on_device(): product, rhs_tile = lax.psum((local_product, local_tile), 'com')]
    all_gather x1 -> x0, waiting for transfers between devices: 84.9 us -> none  [on_device(): gathered = lax.all_gather(transformed, 'arc', axis=2, tiled=True)]
    ppermute x0 -> x57, starting transfers between devices: none -> 77.9 us  [swap(): return lax.ppermute(value, axis, [(i, i ^ bits) for i in range(size)])]
    pallas_call x0 -> x8, Pallas kernels: none -> 38.8 us  [the longest x6 17.3 us: piece_call(): pl.pallas_call(kernel, out_shape=jax.ShapeDtypeStruct(shape, jnp.float32)...]
    another operation x22 -> x0, matrix products: 31 us -> none  [the longest x11 21.8 us: on_device(): transformed = solve_lower(lfactor, coupling).astype(jnp.bfloat16)]
  transfers between devices with their start and end apart: 4 -> 57, of which waited for: 4 -> 25; matrix products, arithmetic and copies ran while one was open for 1% -> 19% of each run, Pallas kernels for 0% -> 12%
where the time goes in v1:
time: 342 us; the launch traced here: 336 us
  waiting for transfers between devices  139 us (41%)
  starting transfers between devices  77.9 us (23%)
  Pallas kernels  38.8 us (11%)
  other arithmetic  31.1 us (9%)
  matrix products  25.2 us (7%)
  local copies, waits for them, and re-layouts  21.6 us (6%)
    ppermute x57, waiting for transfers between devices, swap(): return lax.ppermute(value, axis, [(i, i ^ bits) for i in range(size)])  139 us
    ppermute x57, starting transfers between devices, swap(): return lax.ppermute(value, axis, [(i, i ^ bits) for i in range(size)])  77.9 us
    dot_general x16, matrix products, tdot(): lax.dot_general(a, b, (((0,), (0,)), ((), ())), preferred_element_type=jn...  25.2 us
    pallas_call x6, Pallas kernels, piece_call(): pl.pallas_call(kernel, out_shape=jax.ShapeDtypeStruct(shape, jnp.float32)...  17.3 us
    pallas_call x1, Pallas kernels, forward_solve(): pl.pallas_call(forward_kernel, grid=(arcs // tile,), in_specs=[pl.BlockSp...  16.8 us
    unnamed x132, local copies, waits for them, and re-layouts  12.4 us
    unnamed x45, other arithmetic  9.24 us
  transfers between devices with their start and end apart: 57, of which 25 were waited for; matrix products, arithmetic and copies ran while one was open for 19% of the time, Pallas kernels for 12%

profile of v1, /device:TPU:0, one launch (start us, length us, event | category | flops | bytes accessed | tf_op | source)
XLA Modules:
  0.0 336.4 jit_solution(8075546363272876510)
XLA Ops:
  1.9 2.4 collective-permute-start.46
  6.8 16.8 %shard_map.76 = (bf16[1536,1024]{1,0:T(8,128)(2,1)S(1)}, f32[2,768,128]{2,1,0:T(8,128)S(1)}, f32[256,1024]{1,0:T(8,128)S(1)}) custom-call(f32[2,768,768]{2,1,0:T(8,128)} %factor_ref.3, f32[2,768,1024]{2,1,0:T(8,128)} %links_ref.1, s32[2,1,1024]{2,1,0:T(1,128)S(1)} %reshape.122.usage_ref, bf16[2,768,256]{2,1,0:T(8,128)(2,1)S(1)} %copy-done.8), custom_call_target="tpu_custom_call" | custom-call | flops 7247757312 | bytes 14155776 | tf_op jit(solution)/shard_map/pallas_call | solution.py:109
  26.5 1.5 collective-permute-start.5
  28.0 1.8 constant_dynamic-slice_fusion.50
  31.7 2.2 pad_maximum_fusion.11
  34.8 5.9 %collective-permute-done.5 = f32[4,256,128]{2,1,0:T(8,128)} collective-permute-done((f32[4,256,128]{2,1,0:T(8,128)}, f32[4,256,128]{2,1,0:T(8,128)}, u32[]{:S(2)}, u32[]{:S(2)}) %collective-permute-start.5) | collective-permute-done | bytes 524320 | tf_op jit(solution)/shard_map/ppermute | solution.py:189
  43.5 1.8 collective-permute-start.6
  45.3 2.5 collective-permute-start.8
  50.3 4.9 %collective-permute-done.8 = f32[256,128]{1,0:T(8,128)} collective-permute-done((f32[256,128]{1,0:T(8,128)}, f32[256,128]{1,0:T(8,128)}, u32[]{:S(2)}, u32[]{:S(2)}) %collective-permute-start.8) | collective-permute-done | bytes 131104 | tf_op jit(solution)/shard_map/ppermute | solution.py:189
  55.2 1.6 collective-permute-start.14
  56.7 2.7 collective-permute-done.7
  61.2 1.7 collective-permute-start.18
  64.7 7.3 %collective-permute-done.18 = f32[64,128]{1,0:T(8,128)S(1)} collective-permute-done((f32[64,128]{1,0:T(8,128)S(1)}, f32[64,128]{1,0:T(8,128)S(1)}, u32[]{:S(2)}, u32[]{:S(2)}) %collective-permute-start.18) | collective-permute-done | bytes 32800 | tf_op jit(solution)/shard_map/ppermute | solution.py:189
  73.1 3.0 collective-permute-start.21
  77.6 1.7 collective-permute-done.21
  79.3 1.6 collective-permute-start.2
  82.7 1.6 collective-permute-start.32
  85.4 14.4 %collective-permute-done.2 = bf16[1536,256]{1,0:T(8,128)(2,1)S(1)} collective-permute-done((bf16[1536,256]{1,0:T(8,128)(2,1)S(1)}, bf16[1536,256]{1,0:T(8,128)(2,1)S(1)}, u32[]{:S(2)}, u32[]{:S(2)}) %collective-permute-start.2) | collective-permute-done | bytes 786464 | tf_op jit(solution)/shard_map/ppermute | solution.py:189
  99.8 1.6 collective-permute-start.13
  101.4 1.5 collective-permute-start.29
  104.3 1.8 convolution_convert_fusion.3
  107.2 1.8 convolution_convert_fusion.1
  114.5 7.7 %collective-permute-done.1 = bf16[256,1024]{1,0:T(8,128)(2,1)S(1)} collective-permute-done((bf16[256,1024]{1,0:T(8,128)(2,1)S(1)}, bf16[256,1024]{1,0:T(8,128)(2,1)S(1)}, u32[]{:S(2)}, u32[]{:S(2)}) %collective-permute-start.1) | collective-permute-done | bytes 524320 | tf_op jit(solution)/shard_map/ppermute | solution.py:189
  125.7 5.6 %collective-permute-done.22 = bf16[4,4,64,128]{3,2,1,0:T(8,128)(2,1)S(1)} collective-permute-done((bf16[4,4,64,128]{3,2,1,0:T(8,128)(2,1)S(1)}, bf16[4,4,64,128]{3,2,1,0:T(8,128)(2,1)S(1)}, u32[]{:S(2)}, u32[]{:S(2)}) %collective-permute-start.22) | collective-permute-done | bytes 262176 | tf_op jit(solution)/shard_map/ppermute | solution.py:189
  135.5 9.9 %collective-permute-done.23 = bf16[256,1024]{1,0:T(8,128)(2,1)S(1)} collective-permute-done((bf16[256,1024]{1,0:T(8,128)(2,1)S(1)}, bf16[256,1024]{1,0:T(8,128)(2,1)S(1)}, u32[]{:S(2)}, u32[]{:S(2)}) %collective-permute-start.23) | collective-permute-done | bytes 524320 | tf_op jit(solution)/shard_map/ppermute | solution.py:189
  146.8 2.4 collective-permute-start.24
  149.1 2.5 collective-permute-start.25
  155.0 7.9 %collective-permute-done.24 = bf16[128,1024]{1,0:T(8,128)(2,1)S(1)} collective-permute-done((bf16[128,1024]{1,0:T(8,128)(2,1)S(1)}, bf16[128,1024]{1,0:T(8,128)(2,1)S(1)}, u32[]{:S(2)}, u32[]{:S(2)}) %collective-permute-start.24) | collective-permute-done | bytes 262176 | tf_op jit(solution)/shard_map/ppermute | solution.py:189
  162.9 7.7 %collective-permute-done.25 = bf16[128,1024]{1,0:T(8,128)(2,1)S(1)} collective-permute-done((bf16[128,1024]{1,0:T(8,128)(2,1)S(1)}, bf16[128,1024]{1,0:T(8,128)(2,1)S(1)}, u32[]{:S(2)}, u32[]{:S(2)}) %collective-permute-start.25) | collective-permute-done | bytes 262176 | tf_op jit(solution)/shard_map/ppermute | solution.py:189
  170.7 6.5 %collective-permute-start.11 = (bf16[128,1024]{1,0:T(8,128)(2,1)S(1)}, bf16[128,1024]{1,0:T(8,128)(2,1)S(1)}, u32[]{:S(2)}, u32[]{:S(2)}) collective-permute-start(bf16[128,1024]{1,0:T(8,128)(2,1)S(1)} %get-tuple-element.41), channel_id=1, source_target_pairs={{0,24},{4,28},{8,16},{12,20},{16,8},{20,12},{24,0},{28,4},{1,25},{... | collective-permute-start | bytes 786440 | tf_op jit(solution)/shard_map/ppermute | solution.py:189
  178.2 1.5 collective-permute-start.39
  179.7 5.1 %collective-permute-done.10 = bf16[128,1024]{1,0:T(8,128)(2,1)S(1)} collective-permute-done((bf16[128,1024]{1,0:T(8,128)(2,1)S(1)}, bf16[128,1024]{1,0:T(8,128)(2,1)S(1)}, u32[]{:S(2)}, u32[]{:S(2)}) %collective-permute-start.10) | collective-permute-done | bytes 262176 | tf_op jit(solution)/shard_map/ppermute | solution.py:189
  189.7 3.1 shard_map.78
  192.8 3.1 shard_map.77
  196.0 2.4 shard_map.80
  198.4 2.4 shard_map.79
  201.2 2.9 collective-permute-done.28
  205.6 1.8 convolution_convert_fusion
  207.5 10.2 %collective-permute-done.34 = f32[4,4,64,128]{3,2,1,0:T(8,128)S(1)} collective-permute-done((f32[4,4,64,128]{3,2,1,0:T(8,128)S(1)}, f32[4,4,64,128]{3,2,1,0:T(8,128)S(1)}, u32[]{:S(2)}, u32[]{:S(2)}) %collective-permute-start.34) | collective-permute-done | bytes 524320 | tf_op jit(solution)/shard_map/ppermute | solution.py:189
  217.8 5.2 %collective-permute-start.47 = (f32[4,64,128]{2,1,0:T(8,128)S(1)}, f32[4,64,128]{2,1,0:T(8,128)S(1)}, u32[]{:S(2)}, u32[]{:S(2)}) collective-permute-start(f32[4,64,128]{2,1,0:T(8,128)S(1)} %get-tuple-element.61), channel_id=1, source_target_pairs={{0,8},{4,12},{8,0},{12,4},{16,24},{20,28},{24,16},{28,20},{1,9},{5... | collective-permute-start | bytes 393224 | tf_op jit(solution)/shard_map/ppermute | solution.py:189
  223.0 2.3 collective-permute-start.48
  226.7 1.8 convolution_convert_fusion.2
  228.4 7.4 %collective-permute-done.48 = f32[4,64,128]{2,1,0:T(8,128)S(1)} collective-permute-done((f32[4,64,128]{2,1,0:T(8,128)S(1)}, f32[4,64,128]{2,1,0:T(8,128)S(1)}, u32[]{:S(2)}, u32[]{:S(2)}) %collective-permute-start.48) | collective-permute-done | bytes 131104 | tf_op jit(solution)/shard_map/ppermute | solution.py:189
  236.0 2.0 collective-permute-start.50
  240.5 3.0 convolution_add_fusion.1
  245.4 1.6 collective-permute-start.53
  247.0 3.0 convolution_add_fusion.3
  250.5 2.7 collective-permute-done.53
  262.9 2.1 collective-permute-start.55
  265.2 3.2 shard_map.82
  268.5 3.1 shard_map.81
  272.8 4.7 %shard_map.83 = f32[2,768,64]{2,1,0:T(8,128)S(1)} custom-call(f32[2,768,768]{2,1,0:T(8,128)} %factor_ref.3, f32[2,768,128]{2,1,0:T(8,128)S(1)} %copy-done.7, bf16[2,768,64]{2,1,0:T(8,128)(2,1)S(1)} %constant_dynamic-slice_fusion.32.demand_ref, f32[64,1536]{1,0:T(8,128)S(1)} %add.373.correction_ref), custom_call_target="tpu_custom_call" | custom-call | tf_op jit(solution)/shard_map/pallas_call | solution.py:151
  278.5 2.5 collective-permute-start.40
  281.0 3.0 convolution_add_fusion.2
  284.3 1.6 collective-permute-start.36
  286.0 1.6 collective-permute-start.37
  290.0 3.0 collective-permute-done.40
  296.6 10.8 %collective-permute-done.37 = bf16[128,1024]{1,0:T(8,128)(2,1)S(1)} collective-permute-done((bf16[128,1024]{1,0:T(8,128)(2,1)S(1)}, bf16[128,1024]{1,0:T(8,128)(2,1)S(1)}, u32[]{:S(2)}, u32[]{:S(2)}) %collective-permute-start.37) | collective-permute-done | bytes 262176 | tf_op jit(solution)/shard_map/ppermute | solution.py:189
  307.3 4.4 %collective-permute-start.41 = (bf16[128,1024]{1,0:T(8,128)(2,1)}, bf16[128,1024]{1,0:T(8,128)(2,1)}, u32[]{:S(2)}, u32[]{:S(2)}) collective-permute-start(bf16[128,1024]{1,0:T(8,128)(2,1)} %get-tuple-element.58), channel_id=1, source_target_pairs={{0,8},{4,12},{8,0},{12,4},{16,24},{20,28},{24,16},{28,20},{1,9},{5... | collective-permute-start | bytes 786440 | tf_op jit(solution)/shard_map/ppermute | solution.py:189
  312.5 1.6 collective-permute-start.43
  315.5 1.5 fusion.3
  317.0 3.6 %collective-permute-done.41 = bf16[128,1024]{1,0:T(8,128)(2,1)} collective-permute-done((bf16[128,1024]{1,0:T(8,128)(2,1)}, bf16[128,1024]{1,0:T(8,128)(2,1)}, u32[]{:S(2)}, u32[]{:S(2)}) %collective-permute-start.41) | collective-permute-done | bytes 262176 | tf_op jit(solution)/shard_map/ppermute | solution.py:189
  320.6 12.6 %collective-permute-done.42 = bf16[128,1024]{1,0:T(8,128)(2,1)} collective-permute-done((bf16[128,1024]{1,0:T(8,128)(2,1)}, bf16[128,1024]{1,0:T(8,128)(2,1)}, u32[]{:S(2)}, u32[]{:S(2)}) %collective-permute-start.42) | collective-permute-done | bytes 262176 | tf_op jit(solution)/shard_map/ppermute | solution.py:189
  334.4 1.6 pad_maximum_fusion.4
  (352 shorter events, 79.4 us)
Async XLA Ops:
  1.9 58.7 %collective-permute-start.46 = (f32[128]{0:T(128)}, f32[128]{0:T(128)S(1)}, u32[]{:S(2)}, u32[]{:S(2)}) collective-permute-start(f32[128]{0:T(128)} %get-tuple-element.299), channel_id=1, source_target_pairs={{0,3},{1,2},{2,1},{3,0},{4,7},{5,6},{6,5},{7,4},{8,11},{9,10},{10,... | collective-permute-start | bytes 1544 | tf_op jit(solution)/shard_map/ppermute | solution.py:189
  4.4 58.6 %collective-permute-start.45 = (f32[128]{0:T(128)}, f32[128]{0:T(128)}, u32[]{:S(2)}, u32[]{:S(2)}) collective-permute-start(f32[128]{0:T(128)} %get-tuple-element.299), channel_id=1, source_target_pairs={{0,2},{1,3},{2,0},{3,1},{4,6},{5,7},{6,4},{7,5},{8,10},{9,11},{10,... | collective-permute-start | bytes 1544 | tf_op jit(solution)/shard_map/ppermute | solution.py:189
  24.4 222.5 %copy-start.4 = (bf16[1536,1024]{1,0:T(8,128)(2,1)}, bf16[1536,1024]{1,0:T(8,128)(2,1)S(1)}, u32[]{:S(2)}) copy-start(bf16[1536,1024]{1,0:T(8,128)(2,1)S(1)} %get-tuple-element.36) | copy-start | bytes 9437188
  26.5 14.2 %collective-permute-start.5 = (f32[4,256,128]{2,1,0:T(8,128)}, f32[4,256,128]{2,1,0:T(8,128)}, u32[]{:S(2)}, u32[]{:S(2)}) collective-permute-start(f32[4,256,128]{2,1,0:T(8,128)} %pad_maximum_fusion.25), channel_id=1, source_target_pairs={{0,4},{4,0},{8,12},{12,8},{16,20},{20,16},{24,28},{28,24},{1,5},{5... | collective-permute-start | bytes 1572872 | tf_op jit(solution)/shard_map/ppermute | solution.py:189
  43.5 6.7 %collective-permute-start.6 = (f32[256,128]{1,0:T(8,128)}, f32[256,128]{1,0:T(8,128)}, u32[]{:S(2)}, u32[]{:S(2)}) collective-permute-start(f32[256,128]{1,0:T(8,128)} %get-tuple-element.196), channel_id=1, source_target_pairs={{0,8},{4,12},{8,0},{12,4},{16,24},{20,28},{24,16},{28,20},{1,9},{5... | collective-permute-start | bytes 393224 | tf_op jit(solution)/shard_map/ppermute | solution.py:189
  45.3 9.9 %collective-permute-start.8 = (f32[256,128]{1,0:T(8,128)}, f32[256,128]{1,0:T(8,128)}, u32[]{:S(2)}, u32[]{:S(2)}) collective-permute-start(f32[256,128]{1,0:T(8,128)} %get-tuple-element.197), channel_id=1, source_target_pairs={{0,24},{4,28},{8,16},{12,20},{16,8},{20,12},{24,0},{28,4},{1,25},{... | collective-permute-start | bytes 393224 | tf_op jit(solution)/shard_map/ppermute | solution.py:189
  47.7 11.7 %collective-permute-start.7 = (f32[256,128]{1,0:T(8,128)}, f32[256,128]{1,0:T(8,128)}, u32[]{:S(2)}, u32[]{:S(2)}) collective-permute-start(f32[256,128]{1,0:T(8,128)} %get-tuple-element.198), channel_id=1, source_target_pairs={{0,16},{4,20},{8,24},{12,28},{16,0},{20,4},{24,8},{28,12},{1,17},{... | collective-permute-start | bytes 393224 | tf_op jit(solution)/shard_map/ppermute | solution.py:189
  50.2 13.2 %collective-permute-start.44 = (f32[128]{0:T(128)}, f32[128]{0:T(128)S(1)}, u32[]{:S(2)}, u32[]{:S(2)}) collective-permute-start(f32[128]{0:T(128)} %get-tuple-element.299), channel_id=1, source_target_pairs={{0,1},{1,0},{2,3},{3,2},{4,5},{5,4},{6,7},{7,6},{8,9},{9,8},{10,11... | collective-permute-start | bytes 1544 | tf_op jit(solution)/shard_map/ppermute | solution.py:189
  55.2 27.4 %collective-permute-start.14 = (bf16[1536,256]{1,0:T(8,128)(2,1)}, bf16[1536,256]{1,0:T(8,128)(2,1)S(1)}, u32[]{:S(2)}, u32[]{:S(2)}) collective-permute-start(bf16[1536,256]{1,0:T(8,128)(2,1)} %pad_maximum_fusion.8), channel_id=1, source_target_pairs={{0,2},{1,3},{2,0},{3,1},{4,6},{5,7},{6,4},{7,5},{8,10},{9,11},{10,... | collective-permute-start | bytes 2359304 | tf_op jit(solution)/shard_map/ppermute | solution.py:189
  59.5 23.2 %collective-permute-start.12 = (bf16[1536,256]{1,0:T(8,128)(2,1)}, bf16[1536,256]{1,0:T(8,128)(2,1)S(1)}, u32[]{:S(2)}, u32[]{:S(2)}) collective-permute-start(bf16[1536,256]{1,0:T(8,128)(2,1)} %pad_maximum_fusion.8), channel_id=1, source_target_pairs={{0,1},{1,0},{2,3},{3,2},{4,5},{5,4},{6,7},{7,6},{8,9},{9,8},{10,11... | collective-permute-start | bytes 2359304 | tf_op jit(solution)/shard_map/ppermute | solution.py:189
  61.2 10.7 %collective-permute-start.18 = (f32[64,128]{1,0:T(8,128)S(1)}, f32[64,128]{1,0:T(8,128)S(1)}, u32[]{:S(2)}, u32[]{:S(2)}) collective-permute-start(f32[64,128]{1,0:T(8,128)S(1)} %get-tuple-element.263), channel_id=1, source_target_pairs={{0,3},{1,2},{2,1},{3,0},{4,7},{5,6},{6,5},{7,4},{8,11},{9,10},{10,... | collective-permute-start | bytes 98312 | tf_op jit(solution)/shard_map/ppermute | solution.py:189
  62.9 10.2 %collective-permute-start.17 = (f32[64,128]{1,0:T(8,128)S(1)}, f32[64,128]{1,0:T(8,128)S(1)}, u32[]{:S(2)}, u32[]{:S(2)}) collective-permute-start(f32[64,128]{1,0:T(8,128)S(1)} %get-tuple-element.264), channel_id=1, source_target_pairs={{0,2},{1,3},{2,0},{3,1},{4,6},{5,7},{6,4},{7,5},{8,10},{9,11},{10,... | collective-permute-start | bytes 98312 | tf_op jit(solution)/shard_map/ppermute | solution.py:189
  63.4 9.7 %collective-permute-start.16 = (f32[64,128]{1,0:T(8,128)S(1)}, f32[64,128]{1,0:T(8,128)S(1)}, u32[]{:S(2)}, u32[]{:S(2)}) collective-permute-start(f32[64,128]{1,0:T(8,128)S(1)} %get-tuple-element.265), channel_id=1, source_target_pairs={{0,1},{1,0},{2,3},{3,2},{4,5},{5,4},{6,7},{7,6},{8,9},{9,8},{10,11... | collective-permute-start | bytes 98312 | tf_op jit(solution)/shard_map/ppermute | solution.py:189
  73.1 6.2 %collective-permute-start.21 = (bf16[4,64,128]{2,1,0:T(8,128)(2,1)S(1)}, bf16[4,64,128]{2,1,0:T(8,128)(2,1)S(1)}, u32[]{:S(2)}, u32[]{:S(2)}) collective-permute-start(bf16[4,64,128]{2,1,0:T(8,128)(2,1)S(1)} %fusion.27), channel_id=1, source_target_pairs={{0,24},{4,28},{8,16},{12,20},{16,8},{20,12},{24,0},{28,4},{1,25},{... | collective-permute-start | bytes 196616 | tf_op jit(solution)/shard_map/ppermute | solution.py:189
  76.1 5.6 %collective-permute-start.20 = (bf16[4,64,128]{2,1,0:T(8,128)(2,1)S(1)}, bf16[4,64,128]{2,1,0:T(8,128)(2,1)S(1)}, u32[]{:S(2)}, u32[]{:S(2)}) collective-permute-start(bf16[4,64,128]{2,1,0:T(8,128)(2,1)S(1)} %fusion.27), channel_id=1, source_target_pairs={{0,16},{4,20},{8,24},{12,28},{16,0},{20,4},{24,8},{28,12},{1,17},{... | collective-permute-start | bytes 196616 | tf_op jit(solution)/shard_map/ppermute | solution.py:189
  76.1 5.7 %collective-permute-start.19 = (bf16[4,64,128]{2,1,0:T(8,128)(2,1)S(1)}, bf16[4,64,128]{2,1,0:T(8,128)(2,1)S(1)}, u32[]{:S(2)}, u32[]{:S(2)}) collective-permute-start(bf16[4,64,128]{2,1,0:T(8,128)(2,1)S(1)} %fusion.27), channel_id=1, source_target_pairs={{0,8},{4,12},{8,0},{12,4},{16,24},{20,28},{24,16},{28,20},{1,9},{5... | collective-permute-start | bytes 196616 | tf_op jit(solution)/shard_map/ppermute | solution.py:189
  79.3 20.5 %collective-permute-start.2 = (bf16[1536,256]{1,0:T(8,128)(2,1)S(1)}, bf16[1536,256]{1,0:T(8,128)(2,1)S(1)}, u32[]{:S(2)}, u32[]{:S(2)}) collective-permute-start(bf16[1536,256]{1,0:T(8,128)(2,1)S(1)} %copy-done.49), channel_id=1, source_target_pairs={{0,2},{1,3},{2,0},{3,1},{4,6},{5,7},{6,4},{7,5},{8,10},{9,11},{10,... | collective-permute-start | bytes 2359304 | tf_op jit(solution)/shard_map/ppermute | solution.py:189
  81.8 27.2 %collective-permute-start = (bf16[1536,256]{1,0:T(8,128)(2,1)S(1)}, bf16[1536,256]{1,0:T(8,128)(2,1)S(1)}, u32[]{:S(2)}, u32[]{:S(2)}) collective-permute-start(bf16[1536,256]{1,0:T(8,128)(2,1)S(1)} %copy-done.49), channel_id=1, source_target_pairs={{0,1},{1,0},{2,3},{3,2},{4,5},{5,4},{6,7},{7,6},{8,9},{9,8},{10,11... | collective-permute-start | bytes 2359304 | tf_op jit(solution)/shard_map/ppermute | solution.py:189
  81.8 19.6 %collective-permute-start.27 = (bf16[1536,256]{1,0:T(8,128)(2,1)S(1)}, bf16[1536,256]{1,0:T(8,128)(2,1)S(1)}, u32[]{:S(2)}, u32[]{:S(2)}) collective-permute-start(bf16[1536,256]{1,0:T(8,128)(2,1)S(1)} %copy-done.47), channel_id=1, source_target_pairs={{0,1},{1,0},{2,3},{3,2},{4,5},{5,4},{6,7},{7,6},{8,9},{9,8},{10,11... | collective-permute-start | bytes 2359304 | tf_op jit(solution)/shard_map/ppermute | solution.py:189
  82.6 23.5 %collective-permute-start.31 = (bf16[1536,256]{1,0:T(8,128)(2,1)S(1)}, bf16[1536,256]{1,0:T(8,128)(2,1)S(1)}, u32[]{:S(2)}, u32[]{:S(2)}) collective-permute-start(bf16[1536,256]{1,0:T(8,128)(2,1)S(1)} %copy-done.48), channel_id=1, source_target_pairs={{0,1},{1,0},{2,3},{3,2},{4,5},{5,4},{6,7},{7,6},{8,9},{9,8},{10,11... | collective-permute-start | bytes 2359304 | tf_op jit(solution)/shard_map/ppermute | solution.py:189
  82.7 52.5 %collective-permute-start.32 = (bf16[1536,256]{1,0:T(8,128)(2,1)S(1)}, bf16[1536,256]{1,0:T(8,128)(2,1)S(1)}, u32[]{:S(2)}, u32[]{:S(2)}) collective-permute-start(bf16[1536,256]{1,0:T(8,128)(2,1)S(1)} %copy-done.48), channel_id=1, source_target_pairs={{0,2},{1,3},{2,0},{3,1},{4,6},{5,7},{6,4},{7,5},{8,10},{9,11},{10,... | collective-permute-start | bytes 2359304 | tf_op jit(solution)/shard_map/ppermute | solution.py:189
  99.8 13.3 %collective-permute-start.13 = (bf16[256,1024]{1,0:T(8,128)(2,1)S(1)}, bf16[256,1024]{1,0:T(8,128)(2,1)S(1)}, u32[]{:S(2)}, u32[]{:S(2)}) collective-permute-start(bf16[256,1024]{1,0:T(8,128)(2,1)S(1)} %convolution_convert_fusion.5), channel_id=1, source_target_pairs={{0,4},{4,0},{8,12},{12,8},{16,20},{20,16},{24,28},{28,24},{1,5},{5... | collective-permute-start | bytes 1572872 | tf_op jit(solution)/shard_map/ppermute | solution.py:189
  101.4 34.0 %collective-permute-start.29 = (bf16[1536,256]{1,0:T(8,128)(2,1)S(1)}, bf16[1536,256]{1,0:T(8,128)(2,1)S(1)}, u32[]{:S(2)}, u32[]{:S(2)}) collective-permute-start(bf16[1536,256]{1,0:T(8,128)(2,1)S(1)} %copy-done.47), channel_id=1, source_target_pairs={{0,2},{1,3},{2,0},{3,1},{4,6},{5,7},{6,4},{7,5},{8,10},{9,11},{10,... | collective-permute-start | bytes 2359304 | tf_op jit(solution)/shard_map/ppermute | solution.py:189
  111.0 11.2 %collective-permute-start.1 = (bf16[256,1024]{1,0:T(8,128)(2,1)S(1)}, bf16[256,1024]{1,0:T(8,128)(2,1)S(1)}, u32[]{:S(2)}, u32[]{:S(2)}) collective-permute-start(bf16[256,1024]{1,0:T(8,128)(2,1)S(1)} %convolution_convert_fusion.7), channel_id=1, source_target_pairs={{0,4},{4,0},{8,12},{12,8},{16,20},{20,16},{24,28},{28,24},{1,5},{5... | collective-permute-start | bytes 1572872 | tf_op jit(solution)/shard_map/ppermute | solution.py:189
  111.6 13.0 %collective-permute-start.15 = (bf16[1536,256]{1,0:T(8,128)(2,1)S(1)}, bf16[1536,256]{1,0:T(8,128)(2,1)S(1)}, u32[]{:S(2)}, u32[]{:S(2)}) collective-permute-start(bf16[1536,256]{1,0:T(8,128)(2,1)S(1)} %collective-permute-done.14), channel_id=1, source_target_pairs={{0,1},{1,0},{2,3},{3,2},{4,5},{5,4},{6,7},{7,6},{8,9},{9,8},{10,11... | collective-permute-start | bytes 2359304 | tf_op jit(solution)/shard_map/ppermute | solution.py:189
  112.1 77.6 %copy-start.2 = (bf16[1536,256]{1,0:T(8,128)(2,1)}, bf16[1536,256]{1,0:T(8,128)(2,1)S(1)}, u32[]{:S(2)}) copy-start(bf16[1536,256]{1,0:T(8,128)(2,1)S(1)} %get-tuple-element.306.refs_6_) | copy-start | bytes 2359300
  112.1 80.7 %copy-start = (bf16[1536,256]{1,0:T(8,128)(2,1)}, bf16[1536,256]{1,0:T(8,128)(2,1)S(1)}, u32[]{:S(2)}) copy-start(bf16[1536,256]{1,0:T(8,128)(2,1)S(1)} %get-tuple-element.307.refs_6_) | copy-start | bytes 2359300
  113.1 19.6 %collective-permute-start.3 = (bf16[1536,256]{1,0:T(8,128)(2,1)S(1)}, bf16[1536,256]{1,0:T(8,128)(2,1)S(1)}, u32[]{:S(2)}, u32[]{:S(2)}) collective-permute-start(bf16[1536,256]{1,0:T(8,128)(2,1)S(1)} %collective-permute-done.2), channel_id=1, source_target_pairs={{0,1},{1,0},{2,3},{3,2},{4,5},{5,4},{6,7},{7,6},{8,9},{9,8},{10,11... | collective-permute-start | bytes 2359304 | tf_op jit(solution)/shard_map/ppermute | solution.py:189
  122.2 9.2 %collective-permute-start.22 = (bf16[4,4,64,128]{3,2,1,0:T(8,128)(2,1)S(1)}, bf16[4,4,64,128]{3,2,1,0:T(8,128)(2,1)S(1)}, u32[]{:S(2)}, u32[]{:S(2)}) collective-permute-start(bf16[4,4,64,128]{3,2,1,0:T(8,128)(2,1)S(1)} %pad_maximum_fusion.29), channel_id=1, source_target_pairs={{0,4},{4,0},{8,12},{12,8},{16,20},{20,16},{24,28},{28,24},{1,5},{5... | collective-permute-start | bytes 786440 | tf_op jit(solution)/shard_map/ppermute | solution.py:189
  131.4 14.0 %collective-permute-start.23 = (bf16[256,1024]{1,0:T(8,128)(2,1)S(1)}, bf16[256,1024]{1,0:T(8,128)(2,1)S(1)}, u32[]{:S(2)}, u32[]{:S(2)}) collective-permute-start(bf16[256,1024]{1,0:T(8,128)(2,1)S(1)} %convolution_convert_fusion.4), channel_id=1, source_target_pairs={{0,4},{4,0},{8,12},{12,8},{16,20},{20,16},{24,28},{28,24},{1,5},{5... | collective-permute-start | bytes 1572872 | tf_op jit(solution)/shard_map/ppermute | solution.py:189
  133.8 19.2 %collective-permute-start.4 = (bf16[256,1024]{1,0:T(8,128)(2,1)S(1)}, bf16[256,1024]{1,0:T(8,128)(2,1)S(1)}, u32[]{:S(2)}, u32[]{:S(2)}) collective-permute-start(bf16[256,1024]{1,0:T(8,128)(2,1)S(1)} %convolution_convert_fusion.6), channel_id=1, source_target_pairs={{0,4},{4,0},{8,12},{12,8},{16,20},{20,16},{24,28},{28,24},{1,5},{5... | collective-permute-start | bytes 1572872 | tf_op jit(solution)/shard_map/ppermute | solution.py:189
  135.3 52.0 %copy-start.27 = (bf16[1536,128]{1,0:T(8,128)(2,1)}, bf16[1536,128]{1,0:T(8,128)(2,1)S(1)}, u32[]{:S(2)}) copy-start(bf16[1536,128]{1,0:T(8,128)(2,1)S(1)} %get-tuple-element.137) | copy-start | bytes 1179652
  135.3 52.0 %copy-start.39 = (bf16[1536,128]{1,0:T(8,128)(2,1)}, bf16[1536,128]{1,0:T(8,128)(2,1)S(1)}, u32[]{:S(2)}) copy-start(bf16[1536,128]{1,0:T(8,128)(2,1)S(1)} %get-tuple-element.138) | copy-start | bytes 1179652
  135.3 51.9 %collective-permute-start.33 = (bf16[1536,256]{1,0:T(8,128)(2,1)S(1)}, bf16[1536,256]{1,0:T(8,128)(2,1)S(1)}, u32[]{:S(2)}, u32[]{:S(2)}) collective-permute-start(bf16[1536,256]{1,0:T(8,128)(2,1)S(1)} %collective-permute-done.32), channel_id=1, source_target_pairs={{0,1},{1,0},{2,3},{3,2},{4,5},{5,4},{6,7},{7,6},{8,9},{9,8},{10,11... | collective-permute-start | bytes 2359304 | tf_op jit(solution)/shard_map/ppermute | solution.py:189
  135.5 53.3 %copy-start.29 = (bf16[1536,128]{1,0:T(8,128)(2,1)}, bf16[1536,128]{1,0:T(8,128)(2,1)S(1)}, u32[]{:S(2)}) copy-start(bf16[1536,128]{1,0:T(8,128)(2,1)S(1)} %get-tuple-element.145) | copy-start | bytes 1179652
  135.5 53.3 %copy-start.37 = (bf16[1536,128]{1,0:T(8,128)(2,1)}, bf16[1536,128]{1,0:T(8,128)(2,1)S(1)}, u32[]{:S(2)}) copy-start(bf16[1536,128]{1,0:T(8,128)(2,1)S(1)} %get-tuple-element.146) | copy-start | bytes 1179652
  146.8 16.2 %collective-permute-start.24 = (bf16[128,1024]{1,0:T(8,128)(2,1)S(1)}, bf16[128,1024]{1,0:T(8,128)(2,1)S(1)}, u32[]{:S(2)}, u32[]{:S(2)}) collective-permute-start(bf16[128,1024]{1,0:T(8,128)(2,1)S(1)} %get-tuple-element.45), channel_id=1, source_target_pairs={{0,8},{4,12},{8,0},{12,4},{16,24},{20,28},{24,16},{28,20},{1,9},{5... | collective-permute-start | bytes 786440 | tf_op jit(solution)/shard_map/ppermute | solution.py:189
  149.1 21.5 %collective-permute-start.25 = (bf16[128,1024]{1,0:T(8,128)(2,1)S(1)}, bf16[128,1024]{1,0:T(8,128)(2,1)S(1)}, u32[]{:S(2)}, u32[]{:S(2)}) collective-permute-start(bf16[128,1024]{1,0:T(8,128)(2,1)S(1)} %get-tuple-element.46), channel_id=1, source_target_pairs={{0,16},{4,20},{8,24},{12,28},{16,0},{20,4},{24,8},{28,12},{1,17},{... | collective-permute-start | bytes 786440 | tf_op jit(solution)/shard_map/ppermute | solution.py:189
  151.6 25.6 %collective-permute-start.26 = (bf16[128,1024]{1,0:T(8,128)(2,1)S(1)}, bf16[128,1024]{1,0:T(8,128)(2,1)S(1)}, u32[]{:S(2)}, u32[]{:S(2)}) collective-permute-start(bf16[128,1024]{1,0:T(8,128)(2,1)S(1)} %get-tuple-element.47), channel_id=1, source_target_pairs={{0,24},{4,28},{8,16},{12,20},{16,8},{20,12},{24,0},{28,4},{1,25},{... | collective-permute-start | bytes 786440 | tf_op jit(solution)/shard_map/ppermute | solution.py:189
  154.4 23.9 %collective-permute-start.9 = (bf16[128,1024]{1,0:T(8,128)(2,1)S(1)}, bf16[128,1024]{1,0:T(8,128)(2,1)S(1)}, u32[]{:S(2)}, u32[]{:S(2)}) collective-permute-start(bf16[128,1024]{1,0:T(8,128)(2,1)S(1)} %get-tuple-element.39), channel_id=1, source_target_pairs={{0,8},{4,12},{8,0},{12,4},{16,24},{20,28},{24,16},{28,20},{1,9},{5... | collective-permute-start | bytes 786440 | tf_op jit(solution)/shard_map/ppermute | solution.py:189
  162.9 21.9 %collective-permute-start.10 = (bf16[128,1024]{1,0:T(8,128)(2,1)S(1)}, bf16[128,1024]{1,0:T(8,128)(2,1)S(1)}, u32[]{:S(2)}, u32[]{:S(2)}) collective-permute-start(bf16[128,1024]{1,0:T(8,128)(2,1)S(1)} %get-tuple-element.40), channel_id=1, source_target_pairs={{0,16},{4,20},{8,24},{12,28},{16,0},{20,4},{24,8},{28,12},{1,17},{... | collective-permute-start | bytes 786440 | tf_op jit(solution)/shard_map/ppermute | solution.py:189
  170.7 15.6 %collective-permute-start.11 = (bf16[128,1024]{1,0:T(8,128)(2,1)S(1)}, bf16[128,1024]{1,0:T(8,128)(2,1)S(1)}, u32[]{:S(2)}, u32[]{:S(2)}) collective-permute-start(bf16[128,1024]{1,0:T(8,128)(2,1)S(1)} %get-tuple-element.41), channel_id=1, source_target_pairs={{0,24},{4,28},{8,16},{12,20},{16,8},{20,12},{24,0},{28,4},{1,25},{... | collective-permute-start | bytes 786440 | tf_op jit(solution)/shard_map/ppermute | solution.py:189
  177.2 11.5 %collective-permute-start.30 = (bf16[1536,256]{1,0:T(8,128)(2,1)S(1)}, bf16[1536,256]{1,0:T(8,128)(2,1)S(1)}, u32[]{:S(2)}, u32[]{:S(2)}) collective-permute-start(bf16[1536,256]{1,0:T(8,128)(2,1)S(1)} %collective-permute-done.29), channel_id=1, source_target_pairs={{0,1},{1,0},{2,3},{3,2},{4,5},{5,4},{6,7},{7,6},{8,9},{9,8},{10,11... | collective-permute-start | bytes 2359304 | tf_op jit(solution)/shard_map/ppermute | solution.py:189
  178.2 62.3 %collective-permute-start.39 = (bf16[256,1024]{1,0:T(8,128)(2,1)}, bf16[256,1024]{1,0:T(8,128)(2,1)}, u32[]{:S(2)}, u32[]{:S(2)}) collective-permute-start(bf16[256,1024]{1,0:T(8,128)(2,1)} %convolution_convert_fusion.1), channel_id=1, source_target_pairs={{0,4},{4,0},{8,12},{12,8},{16,20},{20,16},{24,28},{28,24},{1,5},{5... | collective-permute-start | bytes 1572872 | tf_op jit(solution)/shard_map/ppermute | solution.py:189
  184.8 19.3 %collective-permute-start.28 = (bf16[256,1024]{1,0:T(8,128)(2,1)}, bf16[256,1024]{1,0:T(8,128)(2,1)}, u32[]{:S(2)}, u32[]{:S(2)}) collective-permute-start(bf16[256,1024]{1,0:T(8,128)(2,1)} %convolution_convert_fusion.3), channel_id=1, source_target_pairs={{0,4},{4,0},{8,12},{12,8},{16,20},{20,16},{24,28},{28,24},{1,5},{5... | collective-permute-start | bytes 1572872 | tf_op jit(solution)/shard_map/ppermute | solution.py:189
  204.1 13.5 %collective-permute-start.34 = (f32[4,4,64,128]{3,2,1,0:T(8,128)S(1)}, f32[4,4,64,128]{3,2,1,0:T(8,128)S(1)}, u32[]{:S(2)}, u32[]{:S(2)}) collective-permute-start(f32[4,4,64,128]{3,2,1,0:T(8,128)S(1)} %pad_maximum_fusion.26), channel_id=1, source_target_pairs={{0,4},{4,0},{8,12},{12,8},{16,20},{20,16},{24,28},{28,24},{1,5},{5... | collective-permute-start | bytes 1572872 | tf_op jit(solution)/shard_map/ppermute | solution.py:189
  217.8 10.6 %collective-permute-start.47 = (f32[4,64,128]{2,1,0:T(8,128)S(1)}, f32[4,64,128]{2,1,0:T(8,128)S(1)}, u32[]{:S(2)}, u32[]{:S(2)}) collective-permute-start(f32[4,64,128]{2,1,0:T(8,128)S(1)} %get-tuple-element.61), channel_id=1, source_target_pairs={{0,8},{4,12},{8,0},{12,4},{16,24},{20,28},{24,16},{28,20},{1,9},{5... | collective-permute-start | bytes 393224 | tf_op jit(solution)/shard_map/ppermute | solution.py:189
  223.0 12.9 %collective-permute-start.48 = (f32[4,64,128]{2,1,0:T(8,128)S(1)}, f32[4,64,128]{2,1,0:T(8,128)S(1)}, u32[]{:S(2)}, u32[]{:S(2)}) collective-permute-start(f32[4,64,128]{2,1,0:T(8,128)S(1)} %get-tuple-element.62), channel_id=1, source_target_pairs={{0,16},{4,20},{8,24},{12,28},{16,0},{20,4},{24,8},{28,12},{1,17},{... | collective-permute-start | bytes 393224 | tf_op jit(solution)/shard_map/ppermute | solution.py:189
  225.3 10.6 %collective-permute-start.49 = (f32[4,64,128]{2,1,0:T(8,128)S(1)}, f32[4,64,128]{2,1,0:T(8,128)S(1)}, u32[]{:S(2)}, u32[]{:S(2)}) collective-permute-start(f32[4,64,128]{2,1,0:T(8,128)S(1)} %get-tuple-element.63), channel_id=1, source_target_pairs={{0,24},{4,28},{8,16},{12,20},{16,8},{20,12},{24,0},{28,4},{1,25},{... | collective-permute-start | bytes 393224 | tf_op jit(solution)/shard_map/ppermute | solution.py:189
  236.0 7.6 %collective-permute-start.50 = (bf16[4,64,128]{2,1,0:T(8,128)(2,1)S(1)}, bf16[4,64,128]{2,1,0:T(8,128)(2,1)S(1)}, u32[]{:S(2)}, u32[]{:S(2)}) collective-permute-start(bf16[4,64,128]{2,1,0:T(8,128)(2,1)S(1)} %fusion.24), channel_id=1, source_target_pairs={{0,8},{4,12},{8,0},{12,4},{16,24},{20,28},{24,16},{28,20},{1,9},{5... | collective-permute-start | bytes 196616 | tf_op jit(solution)/shard_map/ppermute | solution.py:189
  238.0 6.4 %collective-permute-start.51 = (bf16[4,64,128]{2,1,0:T(8,128)(2,1)S(1)}, bf16[4,64,128]{2,1,0:T(8,128)(2,1)S(1)}, u32[]{:S(2)}, u32[]{:S(2)}) collective-permute-start(bf16[4,64,128]{2,1,0:T(8,128)(2,1)S(1)} %fusion.24), channel_id=1, source_target_pairs={{0,16},{4,20},{8,24},{12,28},{16,0},{20,4},{24,8},{28,12},{1,17},{... | collective-permute-start | bytes 196616 | tf_op jit(solution)/shard_map/ppermute | solution.py:189
  239.1 6.1 %collective-permute-start.52 = (bf16[4,64,128]{2,1,0:T(8,128)(2,1)S(1)}, bf16[4,64,128]{2,1,0:T(8,128)(2,1)S(1)}, u32[]{:S(2)}, u32[]{:S(2)}) collective-permute-start(bf16[4,64,128]{2,1,0:T(8,128)(2,1)S(1)} %fusion.24), channel_id=1, source_target_pairs={{0,24},{4,28},{8,16},{12,20},{16,8},{20,12},{24,0},{28,4},{1,25},{... | collective-permute-start | bytes 196616 | tf_op jit(solution)/shard_map/ppermute | solution.py:189
  245.4 7.8 %collective-permute-start.53 = (bf16[4,4,64,128]{3,2,1,0:T(8,128)(2,1)S(1)}, bf16[4,4,64,128]{3,2,1,0:T(8,128)(2,1)S(1)}, u32[]{:S(2)}, u32[]{:S(2)}) collective-permute-start(bf16[4,4,64,128]{3,2,1,0:T(8,128)(2,1)S(1)} %pad_maximum_fusion.31), channel_id=1, source_target_pairs={{0,4},{4,0},{8,12},{12,8},{16,20},{20,16},{24,28},{28,24},{1,5},{5... | collective-permute-start | bytes 786440 | tf_op jit(solution)/shard_map/ppermute | solution.py:189
  250.0 28.5 %collective-permute-start.35 = (bf16[256,1024]{1,0:T(8,128)(2,1)}, bf16[256,1024]{1,0:T(8,128)(2,1)}, u32[]{:S(2)}, u32[]{:S(2)}) collective-permute-start(bf16[256,1024]{1,0:T(8,128)(2,1)} %convolution_convert_fusion.2), channel_id=1, source_target_pairs={{0,4},{4,0},{8,12},{12,8},{16,20},{20,16},{24,28},{28,24},{1,5},{5... | collective-permute-start | bytes 1572872 | tf_op jit(solution)/shard_map/ppermute | solution.py:189
  262.9 23.1 %collective-permute-start.56 = (bf16[64,1024]{1,0:T(8,128)(2,1)}, bf16[64,1024]{1,0:T(8,128)(2,1)}, u32[]{:S(2)}, u32[]{:S(2)}) collective-permute-start(bf16[64,1024]{1,0:T(8,128)(2,1)} %constant_dynamic-update-slice_fusion.40), channel_id=1, source_target_pairs={{0,3},{1,2},{2,1},{3,0},{4,7},{5,6},{6,5},{7,4},{8,11},{9,10},{10,... | collective-permute-start | bytes 393224 | tf_op jit(solution)/shard_map/ppermute | solution.py:189
  262.9 24.7 %collective-permute-start.54 = (bf16[64,1024]{1,0:T(8,128)(2,1)}, bf16[64,1024]{1,0:T(8,128)(2,1)}, u32[]{:S(2)}, u32[]{:S(2)}) collective-permute-start(bf16[64,1024]{1,0:T(8,128)(2,1)} %get-tuple-element.219), channel_id=1, source_target_pairs={{0,1},{1,0},{2,3},{3,2},{4,5},{5,4},{6,7},{7,6},{8,9},{9,8},{10,11... | collective-permute-start | bytes 393224 | tf_op jit(solution)/shard_map/ppermute | solution.py:189
  262.9 25.9 %collective-permute-start.55 = (bf16[64,1024]{1,0:T(8,128)(2,1)}, bf16[64,1024]{1,0:T(8,128)(2,1)}, u32[]{:S(2)}, u32[]{:S(2)}) collective-permute-start(bf16[64,1024]{1,0:T(8,128)(2,1)} %get-tuple-element.222), channel_id=1, source_target_pairs={{0,2},{1,3},{2,0},{3,1},{4,6},{5,7},{6,4},{7,5},{8,10},{9,11},{10,... | collective-permute-start | bytes 393224 | tf_op jit(solution)/shard_map/ppermute | solution.py:189
  278.5 14.5 %collective-permute-start.40 = (bf16[256,1024]{1,0:T(8,128)(2,1)}, bf16[256,1024]{1,0:T(8,128)(2,1)S(1)}, u32[]{:S(2)}, u32[]{:S(2)}) collective-permute-start(bf16[256,1024]{1,0:T(8,128)(2,1)} %convolution_convert_fusion), channel_id=1, source_target_pairs={{0,4},{4,0},{8,12},{12,8},{16,20},{20,16},{24,28},{28,24},{1,5},{5... | collective-permute-start | bytes 1572872 | tf_op jit(solution)/shard_map/ppermute | solution.py:189
  284.3 12.3 %collective-permute-start.36 = (bf16[128,1024]{1,0:T(8,128)(2,1)S(1)}, bf16[128,1024]{1,0:T(8,128)(2,1)S(1)}, u32[]{:S(2)}, u32[]{:S(2)}) collective-permute-start(bf16[128,1024]{1,0:T(8,128)(2,1)S(1)} %get-tuple-element.53), channel_id=1, source_target_pairs={{0,8},{4,12},{8,0},{12,4},{16,24},{20,28},{24,16},{28,20},{1,9},{5... | collective-permute-start | bytes 786440 | tf_op jit(solution)/shard_map/ppermute | solution.py:189
  286.0 21.4 %collective-permute-start.37 = (bf16[128,1024]{1,0:T(8,128)(2,1)S(1)}, bf16[128,1024]{1,0:T(8,128)(2,1)S(1)}, u32[]{:S(2)}, u32[]{:S(2)}) collective-permute-start(bf16[128,1024]{1,0:T(8,128)(2,1)S(1)} %get-tuple-element.54), channel_id=1, source_target_pairs={{0,16},{4,20},{8,24},{12,28},{16,0},{20,4},{24,8},{28,12},{1,17},{... | collective-permute-start | bytes 786440 | tf_op jit(solution)/shard_map/ppermute | solution.py:189
  287.5 19.8 %collective-permute-start.38 = (bf16[128,1024]{1,0:T(8,128)(2,1)S(1)}, bf16[128,1024]{1,0:T(8,128)(2,1)S(1)}, u32[]{:S(2)}, u32[]{:S(2)}) collective-permute-start(bf16[128,1024]{1,0:T(8,128)(2,1)S(1)} %get-tuple-element.55), channel_id=1, source_target_pairs={{0,24},{4,28},{8,16},{12,20},{16,8},{20,12},{24,0},{28,4},{1,25},{... | collective-permute-start | bytes 786440 | tf_op jit(solution)/shard_map/ppermute | solution.py:189
  307.3 13.2 %collective-permute-start.41 = (bf16[128,1024]{1,0:T(8,128)(2,1)}, bf16[128,1024]{1,0:T(8,128)(2,1)}, u32[]{:S(2)}, u32[]{:S(2)}) collective-permute-start(bf16[128,1024]{1,0:T(8,128)(2,1)} %get-tuple-element.58), channel_id=1, source_target_pairs={{0,8},{4,12},{8,0},{12,4},{16,24},{20,28},{24,16},{28,20},{1,9},{5... | collective-permute-start | bytes 786440 | tf_op jit(solution)/shard_map/ppermute | solution.py:189
  311.7 21.5 %collective-permute-start.42 = (bf16[128,1024]{1,0:T(8,128)(2,1)}, bf16[128,1024]{1,0:T(8,128)(2,1)}, u32[]{:S(2)}, u32[]{:S(2)}) collective-permute-start(bf16[128,1024]{1,0:T(8,128)(2,1)} %get-tuple-element.59), channel_id=1, source_target_pairs={{0,16},{4,20},{8,24},{12,28},{16,0},{20,4},{24,8},{28,12},{1,17},{... | collective-permute-start | bytes 786440 | tf_op jit(solution)/shard_map/ppermute | solution.py:189
  312.5 20.7 %collective-permute-start.43 = (bf16[128,1024]{1,0:T(8,128)(2,1)S(1)}, bf16[128,1024]{1,0:T(8,128)(2,1)}, u32[]{:S(2)}, u32[]{:S(2)}) collective-permute-start(bf16[128,1024]{1,0:T(8,128)(2,1)S(1)} %get-tuple-element.60), channel_id=1, source_target_pairs={{0,24},{4,28},{8,16},{12,20},{16,8},{20,12},{24,0},{28,4},{1,25},{... | collective-permute-start | bytes 786440 | tf_op jit(solution)/shard_map/ppermute | solution.py:189
  (58 other events, 498.4 us)
